TPU v7x, 512 devices: a whole 4x8x8 slice. The times are simulated.
512 devices in a mesh: frame: 64 (over x, y, z_hi), head: 8 (over z_lo, core).
Axes of the slice: x: 4, y: 8, z: 8 (z_hi: 2, z_lo: 4; z = z_hi * 4 + z_lo), core: 2. Of those that a mesh axis runs over, the one named last changes fastest.
Arguments:
- queries: bfloat16 [49152, 5120], P('frame', 'head'), may hold values from -4.5 to 4.5
- keys: bfloat16 [49152, 5120], P('frame', 'head'), may hold values from -4.5 to 4.5
- values: bfloat16 [49152, 5120], P('frame', 'head'), may hold values from -6 to 6
- image_slots: bfloat16 [64, 2, 512, 5120], P('frame', None, None, 'head'), may hold values from -6 to 6
- owner: int32 [1], replicated, may hold values from 0 to 63
- pattern: int32 [192, 5], P('frame'), may hold values from -1 to 191, as said below
Outputs:
- attended: bfloat16 [49152, 5120], P('frame', 'head')
Inputs may be any that keep to these rules, and one draw needn't show every extreme that they name: `pattern`: entry j of tile t's list is t + j - 2 or -1; entry 2 is always t, and entries that would leave the range 0 to 191 are -1.
All inputs are finite; a program needn't handle non-finite values.
Results may differ from a plain program's by a relative error of at most 0.0035.
Values may be sent and summed in bfloat16 or wider, within the bound.
No kernel may reach another device: no remote copies, remote signals or barrier semaphores. Data moves between devices by JAX's collectives and lax.ppermute only.
A program may use at most 128 MiB of HBM per device.

v0:
```python
import jax
import jax.numpy as jnp
from jax import lax
from jax.sharding import PartitionSpec as P

DH = 128
TILE = 256
REACH = 2
NB = 5


def padded_2(block, sides, width):
    for axis, dim in sides:
        count = lax.axis_size(axis)
        forward = [(i, i + 1) for i in range(count - 1)]
        backward = [(target, source) for source, target in forward]
        low = lax.ppermute(
            lax.slice_in_dim(block, block.shape[dim] - width, None, axis=dim), axis, forward
        )
        high = lax.ppermute(lax.slice_in_dim(block, 0, width, axis=dim), axis, backward)
        block = jnp.concatenate([low, block, high], axis=dim)
    return block


def broadcast(shard, axis, root):
    mine = lax.axis_index(axis) == root
    return lax.psum(jnp.where(mine, shard, jnp.zeros_like(shard)), axis)


def tile_attend(query, tile_keys, tile_values, valid):
    heads = query.shape[1] // DH
    qh = query.reshape(query.shape[0], heads, DH)
    kh = tile_keys.reshape(tile_keys.shape[0], heads, DH)
    vh = tile_values.reshape(tile_values.shape[0], heads, DH)
    scores = jnp.einsum("qhd,khd->hqk", qh, kh, preferred_element_type=jnp.float32) * (
        1.0 / DH**0.5
    )
    masked = jnp.where(valid[None, None, :], scores, -jnp.inf)
    top = jnp.max(masked, axis=2, keepdims=True)
    weights = jnp.where(valid[None, None, :], jnp.exp(scores - top), 0.0)
    total = jnp.sum(weights, axis=2)
    rounded = weights.astype(jnp.bfloat16)
    summed = jnp.einsum("hqk,khd->qhd", rounded, vh, preferred_element_type=jnp.float32)
    result = summed / jnp.transpose(total)[:, :, None]
    return result.reshape(query.shape[0], heads * DH).astype(jnp.bfloat16)


def per_device(queries, keys, values, image_slots, owner, pattern):
    rows, width = queries.shape
    local_tiles = rows // TILE
    stacked = jnp.stack([keys, values])
    padded = padded_2(stacked, (("frame", 1),), REACH * TILE)
    span = local_tiles + 2 * REACH
    both_tiles = padded.reshape(2, span, TILE, width)
    slot = image_slots[0]
    image = broadcast(slot, "frame", owner[0])
    first_tile = lax.axis_index("frame") * local_tiles
    query_tiles = queries.reshape(local_tiles, TILE, width)

    def one_tile(item):
        query, row = item
        index = jnp.clip(row - first_tile + REACH, 0, span - 1)
        tile_keys = jnp.take(both_tiles[0], index, axis=0).reshape(NB * TILE, width)
        tile_values = jnp.take(both_tiles[1], index, axis=0).reshape(NB * TILE, width)
        tile_keys = jnp.concatenate([tile_keys, image[0]], axis=0)
        tile_values = jnp.concatenate([tile_values, image[1]], axis=0)
        valid = jnp.concatenate([jnp.repeat(row >= 0, TILE), jnp.ones((image.shape[1],), bool)])
        return tile_attend(query, tile_keys, tile_values, valid)

    out = lax.map(one_tile, (query_tiles, pattern))
    return out.reshape(rows, width)


def solution(mesh):
    in_specs = (
        P("frame", "head"),
        P("frame", "head"),
        P("frame", "head"),
        P("frame", None, None, "head"),
        P(),
        P("frame", None),
    )
    out_specs = P("frame", "head")
    return jax.shard_map(
        per_device, mesh=mesh, in_specs=in_specs, out_specs=out_specs, check_vma=False
    )
```

profile of v0, /device:TPU:8, one launch (start us, length us, event | category | flops | bytes accessed | tf_op | source)
XLA Modules:
  0.0 1059.2 jit_solution(653020691739833565)
XLA Ops:
  6.5 3.5 fusion.36
  10.1 10.9 %collective-permute-start = (bf16[2,512,640]{2,1,0:T(8,128)(2,1)}, bf16[2,512,640]{2,1,0:T(8,128)(2,1)}, u32[]{:S(2)}, u32[]{:S(2)}) collective-permute-start(bf16[2,512,640]{2,1,0:T(8,128)(2,1)} %get-tuple-element.75), channel_id=1, source_target_pairs={{0,8},{8,16},{16,24},{24,32},{32,40},{40,48},{48,56},{56,64},{64,7... | collective-permute-start | bytes 3932168 | tf_op jit(solution)/shard_map/ppermute | solution.py:17
  21.0 1.9 collective-permute-start.1
  24.3 1.2 select_bitcast_fusion
  25.5 120.9 %collective-permute-done = bf16[2,512,640]{2,1,0:T(8,128)(2,1)} collective-permute-done((bf16[2,512,640]{2,1,0:T(8,128)(2,1)}, bf16[2,512,640]{2,1,0:T(8,128)(2,1)}, u32[]{:S(2)}, u32[]{:S(2)}) %collective-permute-start) | collective-permute-done | bytes 1310752 | tf_op jit(solution)/shard_map/ppermute | solution.py:17
  146.3 1.7 collective-permute-done.1
  148.0 7.3 pad_maximum_fusion
  155.3 744.5 %all-reduce.3.cloned.1.call-done = bf16[2,512,640]{1,2,0:T(8,128)(2,1)} async-done(((bf16[2,512,640]{1,2,0:T(8,128)(2,1)}), bf16[2,512,640]{1,2,0:T(8,128)(2,1)}) %all-reduce.3.cloned.1.call-update) | async-done | bytes 1310736 | tf_op jit(solution)/shard_map/psum | solution.py:27
  899.9 152.5 %while.10 = (s32[]{:T(128)}, bf16[3,256,640]{2,1,0:T(8,128)(2,1)}, bf16[2,7,256,640]{3,2,1,0:T(8,128)(2,1)}, s32[3,5]{1,0:T(4,128)S(1)}, s32[]{:T(128)}, /*index...) while((s32[]{:T(128)}, bf16[3,256,640]{2,1,0:T(8,128)(2,1)}, ...), condition=%wide.region_4.6_spmd, body=%wide.region_1.5_spmd.sunk | while | flops 1201605376 | bytes 83909928 | solution.py:70
  899.9 4.2 slice_bitcast_fusion.3
  904.1 3.7 gather_fusion
  907.8 2.0 gather_fusion.1
  909.8 4.0 broadcast_select_fusion.3
  913.8 3.4 concatenate.26
  917.3 1.4 copy.34
  918.7 1.0 constant_dynamic-slice_fusion.3
  919.9 2.3 fusion.53
  922.5 4.9 fusion.54
  927.6 11.2 %fusion.55 = (f32[5,256]{1,0:T(8,128)S(1)}, bf16[5,256,1792]{2,1,0:T(8,128)(2,1)}) fusion(f32[5,256,1792]{2,1,0:T(8,128)} %fusion.54, pred[1792]{0:T(1024)(128)(4,1)S(1)} %concatenate.27), kind=kOutput, calls=%fused_computation.44.clone.1 | output fusion | flops 16058111 | bytes 13769472 | tf_op jit(solution)/shard_map/while/body/eval_jaxpr/sub | solution.py:40
  938.8 3.4 concatenate.28
  942.2 3.1 copy.35
  945.3 4.4 fusion.56
  950.7 4.2 slice_bitcast_fusion.3
  955.0 3.7 gather_fusion
  958.6 2.0 gather_fusion.1
  960.6 4.0 broadcast_select_fusion.3
  964.7 3.4 concatenate.26
  968.1 1.4 copy.34
  969.5 1.0 constant_dynamic-slice_fusion.3
  970.7 2.3 fusion.53
  973.4 4.9 fusion.54
  978.4 11.2 %fusion.55 = (f32[5,256]{1,0:T(8,128)S(1)}, bf16[5,256,1792]{2,1,0:T(8,128)(2,1)}) fusion(f32[5,256,1792]{2,1,0:T(8,128)} %fusion.54, pred[1792]{0:T(1024)(128)(4,1)S(1)} %concatenate.27), kind=kOutput, calls=%fused_computation.44.clone.1 | output fusion | flops 16058111 | bytes 13769472 | tf_op jit(solution)/shard_map/while/body/eval_jaxpr/sub | solution.py:40
  989.6 3.4 concatenate.28
  993.1 3.1 copy.35
  996.2 4.4 fusion.56
  1001.6 4.2 slice_bitcast_fusion.3
  1005.8 3.7 gather_fusion
  1009.5 2.0 gather_fusion.1
  1011.5 4.0 broadcast_select_fusion.3
  1015.5 3.4 concatenate.26
  1019.0 1.4 copy.34
  1020.4 1.0 constant_dynamic-slice_fusion.3
  1021.6 2.3 fusion.53
  1024.2 4.9 fusion.54
  1029.3 11.2 %fusion.55 = (f32[5,256]{1,0:T(8,128)S(1)}, bf16[5,256,1792]{2,1,0:T(8,128)(2,1)}) fusion(f32[5,256,1792]{2,1,0:T(8,128)} %fusion.54, pred[1792]{0:T(1024)(128)(4,1)S(1)} %concatenate.27), kind=kOutput, calls=%fused_computation.44.clone.1 | output fusion | flops 16058111 | bytes 13769472 | tf_op jit(solution)/shard_map/while/body/eval_jaxpr/sub | solution.py:40
  1040.4 3.4 concatenate.28
  1043.9 3.1 copy.35
  1047.0 4.4 fusion.56
  (54 shorter events, 5.5 us)
Async XLA Ops:
  6.5 893.3 %all-reduce.3.cloned.1.call-start = ((), (), s32[]{:S(2)}) async-start(), calls=%async_computation | async-start | bytes 2621440 | tf_op jit(solution)/shard_map/psum | solution.py:27
  6.5 17.0 %copy-start.4 = (bf16[1,2,512,640]{3,2,1,0:T(8,128)(2,1)S(1)}, bf16[1,2,512,640]{3,2,1,0:T(8,128)(2,1)}, u32[]{:S(2)}) copy-start(bf16[1,2,512,640]{3,2,1,0:T(8,128)(2,1)} %param.13) | copy-start | bytes 3932164
  10.1 136.3 %collective-permute-start = (bf16[2,512,640]{2,1,0:T(8,128)(2,1)}, bf16[2,512,640]{2,1,0:T(8,128)(2,1)}, u32[]{:S(2)}, u32[]{:S(2)}) collective-permute-start(bf16[2,512,640]{2,1,0:T(8,128)(2,1)} %get-tuple-element.75), channel_id=1, source_target_pairs={{0,8},{8,16},{16,24},{24,32},{32,40},{40,48},{48,56},{56,64},{64,7... | collective-permute-start | bytes 3932168 | tf_op jit(solution)/shard_map/ppermute | solution.py:17
  21.0 127.0 %collective-permute-start.1 = (bf16[2,512,640]{2,1,0:T(8,128)(2,1)}, bf16[2,512,640]{2,1,0:T(8,128)(2,1)}, u32[]{:S(2)}, u32[]{:S(2)}) collective-permute-start(bf16[2,512,640]{2,1,0:T(8,128)(2,1)} %get-tuple-element.76), channel_id=1, source_target_pairs={{8,0},{16,8},{24,16},{32,24},{40,32},{48,40},{56,48},{64,56},{72,6... | collective-permute-start | bytes 3932168 | tf_op jit(solution)/shard_map/ppermute | solution.py:20
  24.2 123.8 %copy-start.2 = (bf16[768,640]{1,0:T(8,128)(2,1)S(1)}, bf16[768,640]{1,0:T(8,128)(2,1)}, u32[]{:S(2)}) copy-start(bf16[768,640]{1,0:T(8,128)(2,1)} %param.11) | copy-start | bytes 2949124
  24.2 123.8 %copy-start.3 = (bf16[768,640]{1,0:T(8,128)(2,1)S(1)}, bf16[768,640]{1,0:T(8,128)(2,1)}, u32[]{:S(2)}) copy-start(bf16[768,640]{1,0:T(8,128)(2,1)} %param.12) | copy-start | bytes 2949124
  25.5 874.4 %copy-start.5 = (s32[3,5]{1,0:T(4,128)S(1)}, s32[3,5]{1,0:T(4,128)}, u32[]{:S(2)}) copy-start(s32[3,5]{1,0:T(4,128)} %param.15) | copy-start | bytes 184
  919.7 2.8 copy-start
  942.2 3.1 copy-start.1
  970.5 2.8 copy-start
  993.1 3.1 copy-start.1
  1021.4 2.8 copy-start
  1043.9 3.1 copy-start.1
Sparse Core Ops, SparseCore 0:
  25.6 874.2 all-reduce.2
where the time goes:
time: 1060 us
  waiting for transfers between devices  867 us (82%)
  local copies, waits for them, and re-layouts  79.2 us (7%)
  other arithmetic  57.7 us (5%)
  matrix products  28.1 us (3%)
  between operations  14.1 us (1%)
  starting transfers between devices  12.8 us (1%)
    psum x1, waiting for transfers between devices, broadcast(): return lax.psum(jnp.where(mine, shard, jnp.zeros_like(shard)), axis)  745 us
    ppermute x1, waiting for transfers between devices, padded_2(): lax.ppermute(lax.slice_in_dim(block, block.shape[dim] - width, None, axis...  121 us
    sub x3, other arithmetic, tile_attend(): weights = jnp.where(valid[None, None, :], jnp.exp(scores - top), 0.0)  33.6 us
  transfers between devices with their start and end apart: 3, of which 3 were waited for; matrix products, arithmetic and copies ran while one was open for 1% of the time, Pallas kernels for 0%

commit v1 on v0

v1 whole, which is shorter than its diff:
```python
import jax
import jax.numpy as jnp
from jax import lax
from jax.experimental import pallas as pl
from jax.experimental.pallas import tpu as pltpu
from jax.sharding import PartitionSpec as P

DH = 128
TILE = 256
SCALE = 1.4426950408889634 / DH**0.5
NEG = -1e30
F32 = jnp.float32
BF16 = jnp.bfloat16
NX, NY = 4, 8


def at(x, y, z):
    return (x % NX) * (2 * NY) + (y % NY) * 2 + z


FRAMES = [(x, y, z) for x in range(NX) for y in range(NY) for z in range(2)]
FLIP = [(at(x, y, z), at(x, y, 1 - z)) for x, y, z in FRAMES]
ONWARD = [(f, f + 2) for f in range(0, 62, 2)] + [(f, f - 2) for f in range(3, 64, 2)]
DIAGONAL = [(at(x, y, z), at(x, y + 1 - 2 * z, 1 - z)) for x, y, z in FRAMES]
Y_GROUPS = [[at(x, y, z) for y in range(NY)] for x in range(NX) for z in range(2)]


X_GROUPS = [[at(x, y, z) for x in range(NX)] for y in range(NY) for z in range(2)]


def permute(value, pairs):
    return lax.ppermute(value, "frame", pairs)


def exchange(value, groups):
    return lax.all_to_all(value, "frame", 0, 0, axis_index_groups=groups, tiled=True)


def copies(value, count):
    return jnp.broadcast_to(value[None], (count,) + value.shape)


def scores_of(q, k):
    return lax.dot_general(q, k, (((1,), (1,)), ((), ())), preferred_element_type=F32)


def peak_of(r):
    top = r[:, :DH]
    for i in range(DH, r.shape[1], DH):
        top = jnp.maximum(top, r[:, i : i + DH])
    return top


def attend(q, blocks, state):
    raw = [scores_of(q, k) for k, _, _ in blocks]
    peak = None
    for r, (_, _, bias) in zip(raw, blocks):
        here = peak_of(r) * SCALE + bias
        peak = here if peak is None else jnp.maximum(peak, here)
    top = jnp.max(peak, axis=1, keepdims=True)
    if state is not None:
        top = jnp.maximum(state[0], top)
    both = None
    for r, (_, v, bias) in zip(raw, blocks):
        p = jnp.exp2(r * SCALE - (top - bias)).astype(BF16)
        wide = jnp.concatenate([v, jnp.ones_like(v)], axis=1)
        part = jnp.dot(p, wide, preferred_element_type=F32)
        both = part if both is None else both + part
    total, summed = both[:, DH : DH + 1], both[:, :DH]
    if state is not None:
        fade = jnp.exp2(state[0] - top)
        total, summed = state[1] * fade + total, state[2] * fade + summed
    return top, total, summed


def lanes(rows):
    return lax.broadcasted_iota(jnp.int32, (rows, DH), 1)


def put_stats(ref, rows, h, top, total):
    lane = lanes(TILE)
    old = jnp.where(h == 0, 0.0, ref[rows, :])
    ref[rows, :] = jnp.where(lane == h, top, jnp.where(lane == h + DH // 2, total, old))


def get_stats(ref, rows, h):
    lane, held = lanes(TILE), ref[rows, :]
    top = jnp.sum(jnp.where(lane == h, held, 0.0), axis=1, keepdims=True)
    total = jnp.sum(jnp.where(lane == h + DH // 2, held, 0.0), axis=1, keepdims=True)
    return top, total


def finished(total, summed):
    return (summed * (1.0 / total)).astype(BF16)


def tile_rows(tile):
    return pl.ds(pl.multiple_of(tile * TILE, TILE), TILE)


def pack_kernel(_, *refs):
    count = len(refs) // 3
    for i in range(count):
        refs[2 * count + i][0] = refs[2 * i][...]
        refs[2 * count + i][1] = refs[2 * i + 1][...]


def fan_kernel(one, out):
    out[0] = one[...]


def own_kernel(bias, q, k, v, summed_ref, stats_ref):
    h = pl.program_id(0)
    for t in range(3):
        rows = pl.ds(t * TILE, TILE)
        blocks = [
            (k[pl.ds(u * TILE, TILE), :], v[pl.ds(u * TILE, TILE), :], bias[t, u - t + 2])
            for u in range(3)
        ]
        top, total, summed = attend(q[rows, :], blocks, None)
        summed_ref[rows, :] = summed
        put_stats(stats_ref, rows, h, top, total)


def last_kernel(side, bias, q, summed, stats, image, far, mid, fwd, near, out):
    h, p = pl.program_id(0), side[0]
    image_k = image[:, :, 0].reshape(4 * DH, DH)
    image_v = image[:, :, 1].reshape(4 * DH, DH)
    extra = (
        ((far, 1), (fwd, 0)),
        ((far, 0), (near, 4)),
        ((near, 3), (mid, 4)),
    )
    for r in range(3):
        rows = tile_rows(jnp.where(p == 0, r, 2 - r))
        blocks = [(image_k, image_v, 0.0)]
        blocks += [(pair[0], pair[1], bias[r, j]) for pair, j in extra[r]]
        state = get_stats(stats, rows, h) + (summed[rows, :],)
        _, total, acc = attend(q[rows, :], blocks, state)
        out[rows, :] = finished(total, acc)


def cost(blocks, heads):
    return pl.CostEstimate(flops=blocks * heads, transcendentals=0, bytes_accessed=blocks)


def tied(*values):
    return lax.optimization_barrier(values)


def per_device(queries, keys, values, image_slots, owner, pattern):
    rows, width = queries.shape
    heads = width // DH
    frame = lax.axis_index("frame")
    side = frame & 1
    owner_x, owner_y, owner_z = owner[0] // (2 * NY), (owner[0] // 2) % NY, owner[0] % 2
    sides = side.astype(jnp.int32).reshape(1)
    shown = jnp.where(pattern >= 0, 0.0, NEG).astype(F32)
    mirrored = jnp.where(side == 0, shown, shown[::-1, ::-1])
    smem = pl.BlockSpec(memory_space=pltpu.SMEM)
    anywhere = pl.BlockSpec(memory_space=pl.ANY)
    roomy = pltpu.CompilerParams(vmem_limit_bytes=60 * 2**20)

    def pack(*tiles):
        places = jnp.stack([jnp.broadcast_to(t, ()).astype(jnp.int32) for t in tiles])
        ins = [
            pl.BlockSpec((TILE, width), lambda i, t, n=n: (t[n], 0))
            for n in range(len(tiles))
            for _ in range(2)
        ]
        outs = pl.BlockSpec((2, TILE, width), lambda i, t: (0, 0, 0))
        return pl.pallas_call(
            pack_kernel,
            grid_spec=pltpu.PrefetchScalarGridSpec(
                num_scalar_prefetch=1, grid=(1,), in_specs=ins, out_specs=[outs] * len(tiles)
            ),
            out_shape=[jax.ShapeDtypeStruct((2, TILE, width), BF16)] * len(tiles),
            cost_estimate=cost(1, 1),
            compiler_params=roomy,
            name="pack_tiles",
        )(places, *([keys, values] * len(tiles)))

    def whole(h, *_):
        return (0, h)

    def fixed(h, *_):
        return (0, 0)

    pair = pl.BlockSpec((2, TILE, DH), lambda h, s: (0, 0, h))
    every = pl.BlockSpec((rows, DH), whole)
    every_stats = pl.BlockSpec((rows, DH), fixed)
    state_shape = [
        jax.ShapeDtypeStruct((rows, width), F32),
        jax.ShapeDtypeStruct((rows, DH), F32),
    ]

    far, mid = pack(2 * side, 1)
    far, mid = permute(far, FLIP), permute(mid, FLIP)

    slot = image_slots[0].reshape(2, NX, NY, 512 // (NX * NY), width)
    quarters = exchange(jnp.transpose(slot, (1, 2, 0, 3, 4)), X_GROUPS)
    quarter = lax.dynamic_index_in_dim(quarters, owner_x, 0, keepdims=False)

    def scattered(quarter, q, k, v):
        pieces = exchange(quarter, Y_GROUPS)
        summed, stats = pl.pallas_call(
            own_kernel,
            grid=(heads,),
            in_specs=[smem, every, every, every],
            out_specs=[every, every_stats],
            out_shape=state_shape,
            cost_estimate=cost(9, heads),
            compiler_params=roomy,
            name="own_tiles",
        )(shown, q, k, v)
        pieces, summed, stats = tied(pieces, summed, stats)
        piece = lax.dynamic_index_in_dim(pieces, owner_y, 0, keepdims=False)
        piece = jnp.where(side == owner_z, piece, permute(piece, DIAGONAL))
        return piece, summed, stats

    def nothing(function):
        def run(*operands):
            shapes = jax.eval_shape(function, *operands)
            return jax.tree.map(lambda a: jnp.zeros(a.shape, a.dtype), shapes)

        return run

    always = owner[0] >= 0
    piece, summed, stats = lax.cond(
        always, scattered, nothing(scattered), quarter, queries, keys, values
    )
    column = exchange(copies(piece, NY), Y_GROUPS)
    far = permute(tied(far, piece)[0], ONWARD)
    fwd = permute(tied(mid, piece)[0], ONWARD)
    near = permute(pack(2 - 2 * side)[0], FLIP)

    fan = pl.pallas_call(
        fan_kernel,
        grid=(NX,),
        in_specs=[pl.BlockSpec(column.shape, lambda i: (0, 0, 0, 0))],
        out_specs=pl.BlockSpec((1,) + column.shape, lambda i: (i, 0, 0, 0, 0)),
        out_shape=jax.ShapeDtypeStruct((NX,) + column.shape, BF16),
        cost_estimate=pl.CostEstimate(flops=6 * 10**9, transcendentals=0, bytes_accessed=0),
        compiler_params=roomy,
        name="fan_out",
    )(column)

    def gathered(fan):
        return exchange(fan, X_GROUPS)

    image = lax.cond(always, gathered, nothing(gathered), fan)

    return pl.pallas_call(
        last_kernel,
        grid_spec=pltpu.PrefetchScalarGridSpec(
            num_scalar_prefetch=1,
            grid=(heads,),
            in_specs=[smem, every, every, every_stats]
            + [pl.BlockSpec((NX, NY, 2, 16, DH), lambda h, s: (0, 0, 0, 0, h))]
            + [pair] * 4,
            out_specs=every,
        ),
        out_shape=jax.ShapeDtypeStruct((rows, width), BF16),
        cost_estimate=cost(12, heads),
        compiler_params=roomy,
        name="image_and_halo",
    )(sides, mirrored, queries, summed, stats, image, far, mid, fwd, near)


def solution(mesh):
    in_specs = (
        P("frame", "head"),
        P("frame", "head"),
        P("frame", "head"),
        P("frame", None, None, "head"),
        P(),
        P("frame", None),
    )
    out_specs = P("frame", "head")
    return jax.shard_map(
        per_device, mesh=mesh, in_specs=in_specs, out_specs=out_specs, check_vma=False
    )
```

time: 1060 us -> 137 us (0.13)
  the two profiles are of different devices: /device:TPU:8 before, /device:TPU:1 now
where the time goes in v1:
time: 137 us; the launch traced here: 136 us
  starting transfers between devices  57.4 us (42%)
  blocking collectives  39.2 us (29%)
  Pallas kernels  23.8 us (17%)
  local copies, waits for them, and re-layouts  6.73 us (5%)
  waiting for transfers between devices  5.26 us (4%)
  other arithmetic  1.98 us (1%)
    ppermute x6, starting transfers between devices, permute(): return lax.ppermute(value, 'frame', pairs)  39.5 us
    all_to_all x1, blocking collectives, exchange(): lax.all_to_all(value, 'frame', 0, 0, axis_index_groups=groups, tiled=True)  39.2 us
    all_to_all x3, starting transfers between devices, exchange(): lax.all_to_all(value, 'frame', 0, 0, axis_index_groups=groups, tiled=True)  17.9 us
    pallas_call x1, Pallas kernels, per_device(): pl.pallas_call(last_kernel, grid_spec=pltpu.PrefetchScalarGridSpec(num_sc...  10.2 us
    pallas_call x1, Pallas kernels, scattered(): pl.pallas_call(own_kernel, grid=(heads,), in_specs=[smem, every, every, e...  8.17 us
    all_to_all x3, waiting for transfers between devices, exchange(): lax.all_to_all(value, 'frame', 0, 0, axis_index_groups=groups, tiled=True)  3.3 us
    pallas_call x2, Pallas kernels, pack(): pl.pallas_call(pack_kernel, grid_spec=pltpu.PrefetchScalarGridSpec(num_sc...  2.85 us
  transfers between devices with their start and end apart: 9, of which 2 were waited for; matrix products, arithmetic and copies ran while one was open for 4% of the time, Pallas kernels for 10%

profile of v1, /device:TPU:1, one launch (start us, length us, event | category | flops | bytes accessed | tf_op | source)
XLA Modules:
  0.0 135.8 jit_solution(14598125558939974841)
XLA Ops:
  0.0 2.5 %copy.8 = bf16[4,8,2,16,640]{4,3,1,2,0:T(8,128)(2,1)} copy(bf16[4,8,2,16,640]{4,3,1,0,2:T(8,128)(2,1)} %bitcast.17) | data formatting | bytes 2621440 | tf_op jit(solution)/shard_map/transpose | solution.py:201
  2.5 0.0 copy-start
  2.5 0.0 copy-start.1
  2.5 5.0 %all-to-all-start.2 = ((bf16[4,8,2,16,640]{4,3,1,2,0:T(8,128)(2,1)}), bf16[4,8,2,16,640]{4,3,1,2,0:T(8,128)(2,1)}, u32[]{:S(2)}, u32[]{:S(2)}) async-start(bf16[4,8,2,16,640]{4,3,1,2,0:T(8,128)(2,1)} %copy.8), calls=%async_computation.2 | async-start | bytes 2621440 | tf_op jit(solution)/shard_map/all_to_all | solution.py:36
  7.5 0.6 pad_add_fusion._
  8.1 0.0 copy-done
  8.1 0.0 copy-done.1
  8.1 0.0 copy-start.4
  8.1 0.0 copy-start.2
  8.1 2.0 %pack_tiles.2 = (bf16[2,256,640]{2,1,0:T(8,128)(2,1)}, bf16[2,256,640]{2,1,0:T(8,128)(2,1)}) custom-call(s32[2]{0:T(128)} %pad_add_fusion._, bf16[768,640]{1,0:T(8,128)(2,1)S(1)} %copy-done, bf16[768,640]{1,0:T(8,128)(2,1)S(1)} %copy-done.1, bf16[768,640]{1,0:T(8,128)(2,1)S(1)} %copy-done, bf16[768,640]{1,0:T(8,128)(2,1)S(1)} %copy-done.1), custom_call_target="tpu_custom_call" | custom-call | flops 1 | bytes 1 | tf_op jit(solution)/shard_map/pack_tiles/pallas_call | solution.py:172
  10.1 10.9 %collective-permute-start.1 = (bf16[2,256,640]{2,1,0:T(8,128)(2,1)}, bf16[2,256,640]{2,1,0:T(8,128)(2,1)}, u32[]{:S(2)}, u32[]{:S(2)}) collective-permute-start(bf16[2,256,640]{2,1,0:T(8,128)(2,1)} %get-tuple-element.120), channel_id=1, source_target_pairs={{0,8},{8,0},{16,24},{24,16},{32,40},{40,32},{48,56},{56,48},{64,72... | collective-permute-start | bytes 1966088 | tf_op jit(solution)/shard_map/ppermute | solution.py:32
  21.0 1.9 %collective-permute-start.3 = (bf16[2,256,640]{2,1,0:T(8,128)(2,1)}, bf16[2,256,640]{2,1,0:T(8,128)(2,1)}, u32[]{:S(2)}, u32[]{:S(2)}) collective-permute-start(bf16[2,256,640]{2,1,0:T(8,128)(2,1)} %get-tuple-element.122), channel_id=1, source_target_pairs={{0,8},{8,0},{16,24},{24,16},{32,40},{40,32},{48,56},{56,48},{64,72... | collective-permute-start | bytes 1966088 | tf_op jit(solution)/shard_map/ppermute | solution.py:32
  23.6 0.0 copy-done.4
  23.6 0.0 all-to-all-done.2
  23.6 0.0 copy-done.2
  23.6 35.8 %conditional.2 = (bf16[2,16,640]{2,1,0:T(8,128)(2,1)S(1)}, f32[768,640]{1,0:T(8,128)}, f32[768,128]{1,0:T(8,128)S(1)}) conditional(s32[]{:T(128)} %convert_element_type.4, () %tuple.36, (pred[]{:T(512)}, s32[]{:T(128)}, s32[]{:T(128)}, pred[]{:T(512)}, s32[]{:T(128)}, /*index=5*/bf16[4,8,2,16,640]{4,3,1,2,0:T(8,128)(2,1)}, f32[3,5]{1,0:T(4,128)S(1)}, ...), branch_computations={%region_0.1_spmd, %region_1.2_spmd} | conditional | flops 20568 | bytes 2400290 | solution.py:229
  24.3 1.7 %dynamic-slice_bitcast_fusion = bf16[8,2,16,640]{3,2,1,0:T(8,128)(2,1)} fusion(s32[]{:T(128)S(6)} %select_n.42, bf16[4,8,2,16,640]{4,3,1,2,0:T(8,128)(2,1)} %get-tuple-element.154), kind=kLoop, calls=%fused_computation | loop fusion | bytes 655364 | tf_op jit(solution)/shard_map/jit(dynamic_index_in_dim)/squeeze | solution.py:202
  26.1 8.3 %all-to-all-start.1 = ((bf16[8,2,16,640]{3,2,1,0:T(8,128)(2,1)}), bf16[8,2,16,640]{3,2,1,0:T(8,128)(2,1)}, u32[]{:S(2)}, u32[]{:S(2)}) async-start(bf16[8,2,16,640]{3,2,1,0:T(8,128)(2,1)} %dynamic-slice_bitcast_fusion), calls=%async_computation.1 | async-start | bytes 655360 | tf_op jit(solution)/shard_map/cond/branch_1_fun/all_to_all | solution.py:36
  34.4 8.2 %own_tiles.1 = (f32[768,640]{1,0:T(8,128)}, f32[768,128]{1,0:T(8,128)S(1)}) custom-call(f32[3,5]{1,0:T(4,128)S(1)} %get-tuple-element.100.bias, bf16[768,640]{1,0:T(8,128)(2,1)S(1)} %get-tuple-element.101.q, bf16[768,640]{1,0:T(8,128)(2,1)S(1)} %get-tuple-element.102.k, bf16[768,640]{1,0:T(8,128)(2,1)S(1)} %get-tuple-element.103.v), custom_call_target="tpu_custom_call" | custom-call | flops 45 | bytes 9 | tf_op jit(solution)/shard_map/cond/branch_1_fun/own_tiles/pallas_call | solution.py:206
  42.5 3.3 %all-to-all-done.1 = bf16[8,2,16,640]{3,2,1,0:T(8,128)(2,1)} async-done(((bf16[8,2,16,640]{3,2,1,0:T(8,128)(2,1)}), bf16[8,2,16,640]{3,2,1,0:T(8,128)(2,1)}, u32[]{:S(2)}, u32[]{:S(2)}) %all-to-all-start.1) | async-done | bytes 327712 | tf_op jit(solution)/shard_map/cond/branch_1_fun/all_to_all | solution.py:36
  45.8 0.8 dynamic-slice_bitcast_fusion.1
  46.6 10.1 %collective-permute-start = (bf16[2,16,640]{2,1,0:T(8,128)(2,1)S(1)}, bf16[2,16,640]{2,1,0:T(8,128)(2,1)S(1)}, u32[]{:S(2)}, u32[]{:S(2)}) collective-permute-start(bf16[2,16,640]{2,1,0:T(8,128)(2,1)S(1)} %dynamic-slice_bitcast_fusion.1), channel_id=1, source_target_pairs={{0,24},{8,112},{16,40},{24,0},{32,56},{40,16},{48,72},{56,32},{64,... | collective-permute-start | bytes 122888 | tf_op jit(solution)/shard_map/cond/branch_1_fun/ppermute | solution.py:32
  56.7 2.0 %collective-permute-done = bf16[2,16,640]{2,1,0:T(8,128)(2,1)S(1)} collective-permute-done((bf16[2,16,640]{2,1,0:T(8,128)(2,1)S(1)}, bf16[2,16,640]{2,1,0:T(8,128)(2,1)S(1)}, u32[]{:S(2)}, u32[]{:S(2)}) %collective-permute-start) | collective-permute-done | bytes 40992 | tf_op jit(solution)/shard_map/cond/branch_1_fun/ppermute | solution.py:32
  58.7 0.8 broadcast_select_fusion
  59.5 0.8 broadcast_in_dim.16
  60.2 4.6 %all-to-all-start.3 = ((bf16[8,2,16,640]{3,2,1,0:T(8,128)(2,1)}), bf16[8,2,16,640]{3,2,1,0:T(8,128)(2,1)}, u32[]{:S(2)}, u32[]{:S(2)}) async-start(bf16[8,2,16,640]{3,2,1,0:T(8,128)(2,1)} %broadcast_in_dim.16), calls=%async_computation.3 | async-start | bytes 655360 | tf_op jit(solution)/shard_map/all_to_all | solution.py:36
  64.8 0.9 pack_tiles.3
  65.7 9.4 %collective-permute-start.5 = (bf16[2,256,640]{2,1,0:T(8,128)(2,1)}, bf16[2,256,640]{2,1,0:T(8,128)(2,1)S(1)}, u32[]{:S(2)}, u32[]{:S(2)}) collective-permute-start(bf16[2,256,640]{2,1,0:T(8,128)(2,1)} %pack_tiles.3), channel_id=1, source_target_pairs={{0,8},{8,0},{16,24},{24,16},{32,40},{40,32},{48,56},{56,48},{64,72... | collective-permute-start | bytes 1966088 | tf_op jit(solution)/shard_map/ppermute | solution.py:32
  75.1 0.1 rev.3
  75.2 0.0 collective-permute-done.1
  75.2 4.1 %collective-permute-start.2 = (bf16[2,256,640]{2,1,0:T(8,128)(2,1)}, bf16[2,256,640]{2,1,0:T(8,128)(2,1)}, u32[]{:S(2)}, u32[]{:S(2)}) collective-permute-start(bf16[2,256,640]{2,1,0:T(8,128)(2,1)} %collective-permute-done.1), channel_id=1, source_target_pairs={{0,16},{16,32},{32,48},{48,64},{64,80},{80,96},{96,112},{112,128},... | collective-permute-start | bytes 1966088 | tf_op jit(solution)/shard_map/ppermute | solution.py:32
  79.3 0.0 collective-permute-done.3.mid
  79.3 3.1 %collective-permute-start.4 = (bf16[2,256,640]{2,1,0:T(8,128)(2,1)}, bf16[2,256,640]{2,1,0:T(8,128)(2,1)}, u32[]{:S(2)}, u32[]{:S(2)}) collective-permute-start(bf16[2,256,640]{2,1,0:T(8,128)(2,1)} %collective-permute-done.3.mid), channel_id=1, source_target_pairs={{0,16},{16,32},{32,48},{48,64},{64,80},{80,96},{96,112},{112,128},... | collective-permute-start | bytes 1966088 | tf_op jit(solution)/shard_map/ppermute | solution.py:32
  82.4 0.6 broadcast_select_fusion.1.bias
  83.0 0.0 all-to-all-done.3.one
  83.0 2.6 %fan_out.1 = bf16[4,8,2,16,640]{4,3,2,1,0:T(8,128)(2,1)} custom-call(bf16[8,2,16,640]{3,2,1,0:T(8,128)(2,1)} %all-to-all-done.3.one), custom_call_target="tpu_custom_call" | custom-call | flops 6000000000 | tf_op jit(solution)/shard_map/fan_out/pallas_call | solution.py:237
  85.6 39.2 %conditional.3 = (bf16[4,8,2,16,640]{4,3,2,1,0:T(8,128)(2,1)S(1)}) conditional(s32[]{:T(128)} %convert_element_type.4, () %tuple.38, bf16[4,8,2,16,640]{4,3,2,1,0:T(8,128)(2,1)} %fan_out.1), branch_computations={%region_2.3_spmd, %region_3.4_spmd} | conditional | bytes 2621448 | solution.py:251
  85.6 39.2 %all_to_all.18 = bf16[4,8,2,16,640]{4,3,2,1,0:T(8,128)(2,1)S(1)} all-to-all(bf16[4,8,2,16,640]{4,3,2,1,0:T(8,128)(2,1)} %param.3), channel_id=1, replica_groups={{0,128,256,384},{8,136,264,392},{16,144,272,400},{24,152,280,408},{32,1..., dimensions={0} | all-to-all | bytes 2621440 | tf_op jit(solution)/shard_map/cond/branch_1_fun/all_to_all | solution.py:36
  124.8 0.0 collective-permute-done.5.near
  124.8 0.0 copy-start.3
  124.8 0.0 collective-permute-done.2.far
  124.8 0.0 collective-permute-done.4.fwd
  124.8 0.8 copy-done.3
  125.6 10.2 %image_and_halo.1 = bf16[768,640]{1,0:T(8,128)(2,1)} custom-call(s32[1]{0:T(128)} %bitcast.2.side, f32[3,5]{1,0:T(4,128)} %broadcast_select_fusion.1.bias, bf16[768,640]{1,0:T(8,128)(2,1)S(1)} %copy-done.2, f32[768,640]{1,0:T(8,128)} %get-tuple-element.117.summed, f32[768,128]{1,0:T(8,128)S(1)} %get-tuple-element.118.stats, ...), custom_call_target="tpu_custom_call" | custom-call | flops 60 | bytes 12 | tf_op jit(solution)/shard_map/image_and_halo/pallas_call | solution.py:253
  (1 shorter events, 0.0 us)
Async XLA Ops:
  2.5 5.6 %copy-start = (bf16[768,640]{1,0:T(8,128)(2,1)S(1)}, bf16[768,640]{1,0:T(8,128)(2,1)}, u32[]{:S(2)}) copy-start(bf16[768,640]{1,0:T(8,128)(2,1)} %refs_0_.3) | copy-start | bytes 2949124
  2.5 5.6 %copy-start.1 = (bf16[768,640]{1,0:T(8,128)(2,1)S(1)}, bf16[768,640]{1,0:T(8,128)(2,1)}, u32[]{:S(2)}) copy-start(bf16[768,640]{1,0:T(8,128)(2,1)} %refs_1_.3) | copy-start | bytes 2949124
  2.5 21.1 %all-to-all-start.2 = ((bf16[4,8,2,16,640]{4,3,1,2,0:T(8,128)(2,1)}), bf16[4,8,2,16,640]{4,3,1,2,0:T(8,128)(2,1)}, u32[]{:S(2)}, u32[]{:S(2)}) async-start(bf16[4,8,2,16,640]{4,3,1,2,0:T(8,128)(2,1)} %copy.8), calls=%async_computation.2 | async-start | bytes 2621440 | tf_op jit(solution)/shard_map/all_to_all | solution.py:36
  8.1 15.5 %copy-start.4 = (s32[3,5]{1,0:T(4,128)S(1)}, s32[3,5]{1,0:T(4,128)}, u32[]{:S(2)}) copy-start(s32[3,5]{1,0:T(4,128)} %param.15) | copy-start | bytes 184
  8.1 15.5 %copy-start.2 = (bf16[768,640]{1,0:T(8,128)(2,1)S(1)}, bf16[768,640]{1,0:T(8,128)(2,1)}, u32[]{:S(2)}) copy-start(bf16[768,640]{1,0:T(8,128)(2,1)} %q.1) | copy-start | bytes 2949124
  10.1 65.2 %collective-permute-start.1 = (bf16[2,256,640]{2,1,0:T(8,128)(2,1)}, bf16[2,256,640]{2,1,0:T(8,128)(2,1)}, u32[]{:S(2)}, u32[]{:S(2)}) collective-permute-start(bf16[2,256,640]{2,1,0:T(8,128)(2,1)} %get-tuple-element.120), channel_id=1, source_target_pairs={{0,8},{8,0},{16,24},{24,16},{32,40},{40,32},{48,56},{56,48},{64,72... | collective-permute-start | bytes 1966088 | tf_op jit(solution)/shard_map/ppermute | solution.py:32
  21.0 58.3 %collective-permute-start.3 = (bf16[2,256,640]{2,1,0:T(8,128)(2,1)}, bf16[2,256,640]{2,1,0:T(8,128)(2,1)}, u32[]{:S(2)}, u32[]{:S(2)}) collective-permute-start(bf16[2,256,640]{2,1,0:T(8,128)(2,1)} %get-tuple-element.122), channel_id=1, source_target_pairs={{0,8},{8,0},{16,24},{24,16},{32,40},{40,32},{48,56},{56,48},{64,72... | collective-permute-start | bytes 1966088 | tf_op jit(solution)/shard_map/ppermute | solution.py:32
  26.1 19.8 %all-to-all-start.1 = ((bf16[8,2,16,640]{3,2,1,0:T(8,128)(2,1)}), bf16[8,2,16,640]{3,2,1,0:T(8,128)(2,1)}, u32[]{:S(2)}, u32[]{:S(2)}) async-start(bf16[8,2,16,640]{3,2,1,0:T(8,128)(2,1)} %dynamic-slice_bitcast_fusion), calls=%async_computation.1 | async-start | bytes 655360 | tf_op jit(solution)/shard_map/cond/branch_1_fun/all_to_all | solution.py:36
  46.6 12.1 %collective-permute-start = (bf16[2,16,640]{2,1,0:T(8,128)(2,1)S(1)}, bf16[2,16,640]{2,1,0:T(8,128)(2,1)S(1)}, u32[]{:S(2)}, u32[]{:S(2)}) collective-permute-start(bf16[2,16,640]{2,1,0:T(8,128)(2,1)S(1)} %dynamic-slice_bitcast_fusion.1), channel_id=1, source_target_pairs={{0,24},{8,112},{16,40},{24,0},{32,56},{40,16},{48,72},{56,32},{64,... | collective-permute-start | bytes 122888 | tf_op jit(solution)/shard_map/cond/branch_1_fun/ppermute | solution.py:32
  60.2 22.8 %all-to-all-start.3 = ((bf16[8,2,16,640]{3,2,1,0:T(8,128)(2,1)}), bf16[8,2,16,640]{3,2,1,0:T(8,128)(2,1)}, u32[]{:S(2)}, u32[]{:S(2)}) async-start(bf16[8,2,16,640]{3,2,1,0:T(8,128)(2,1)} %broadcast_in_dim.16), calls=%async_computation.3 | async-start | bytes 655360 | tf_op jit(solution)/shard_map/all_to_all | solution.py:36
  65.7 59.1 %collective-permute-start.5 = (bf16[2,256,640]{2,1,0:T(8,128)(2,1)}, bf16[2,256,640]{2,1,0:T(8,128)(2,1)S(1)}, u32[]{:S(2)}, u32[]{:S(2)}) collective-permute-start(bf16[2,256,640]{2,1,0:T(8,128)(2,1)} %pack_tiles.3), channel_id=1, source_target_pairs={{0,8},{8,0},{16,24},{24,16},{32,40},{40,32},{48,56},{56,48},{64,72... | collective-permute-start | bytes 1966088 | tf_op jit(solution)/shard_map/ppermute | solution.py:32
  75.2 49.5 %collective-permute-start.2 = (bf16[2,256,640]{2,1,0:T(8,128)(2,1)}, bf16[2,256,640]{2,1,0:T(8,128)(2,1)}, u32[]{:S(2)}, u32[]{:S(2)}) collective-permute-start(bf16[2,256,640]{2,1,0:T(8,128)(2,1)} %collective-permute-done.1), channel_id=1, source_target_pairs={{0,16},{16,32},{32,48},{48,64},{64,80},{80,96},{96,112},{112,128},... | collective-permute-start | bytes 1966088 | tf_op jit(solution)/shard_map/ppermute | solution.py:32
  79.3 45.5 %collective-permute-start.4 = (bf16[2,256,640]{2,1,0:T(8,128)(2,1)}, bf16[2,256,640]{2,1,0:T(8,128)(2,1)}, u32[]{:S(2)}, u32[]{:S(2)}) collective-permute-start(bf16[2,256,640]{2,1,0:T(8,128)(2,1)} %collective-permute-done.3.mid), channel_id=1, source_target_pairs={{0,16},{16,32},{32,48},{48,64},{64,80},{80,96},{96,112},{112,128},... | collective-permute-start | bytes 1966088 | tf_op jit(solution)/shard_map/ppermute | solution.py:32
  124.8 0.8 copy-start.3

commit v2 on v1

--- a/solution.py
+++ b/solution.py
@@ -21,6 +21,7 @@
 FRAMES = [(x, y, z) for x in range(NX) for y in range(NY) for z in range(2)]
 FLIP = [(at(x, y, z), at(x, y, 1 - z)) for x, y, z in FRAMES]
 ONWARD = [(f, f + 2) for f in range(0, 62, 2)] + [(f, f - 2) for f in range(3, 64, 2)]
+BEFORE = [(f, f + 2) for f in range(1, 62, 2)] + [(f, f - 2) for f in range(2, 64, 2)]
 DIAGONAL = [(at(x, y, z), at(x, y + 1 - 2 * z, 1 - z)) for x, y, z in FRAMES]
 Y_GROUPS = [[at(x, y, z) for y in range(NY)] for x in range(NX) for z in range(2)]
 
@@ -105,10 +106,6 @@
         refs[2 * count + i][1] = refs[2 * i + 1][...]
 
 
-def fan_kernel(one, out):
-    out[0] = one[...]
-
-
 def own_kernel(bias, q, k, v, summed_ref, stats_ref):
     h = pl.program_id(0)
     for t in range(3):
@@ -120,6 +117,10 @@
         top, total, summed = attend(q[rows, :], blocks, None)
         summed_ref[rows, :] = summed
         put_stats(stats_ref, rows, h, top, total)
+
+
+def hold_kernel(stats, arrived, out):
+    pass
 
 
 def last_kernel(side, bias, q, summed, stats, image, far, mid, fwd, near, out):
@@ -194,14 +195,15 @@
         jax.ShapeDtypeStruct((rows, DH), F32),
     ]
 
-    far, mid = pack(2 * side, 1)
-    far, mid = permute(far, FLIP), permute(mid, FLIP)
+    far, mid, near = pack(2 * side, 1, 2 - 2 * side)
+    mid, near = permute(mid, FLIP), permute(near, FLIP)
 
     slot = image_slots[0].reshape(2, NX, NY, 512 // (NX * NY), width)
     quarters = exchange(jnp.transpose(slot, (1, 2, 0, 3, 4)), X_GROUPS)
     quarter = lax.dynamic_index_in_dim(quarters, owner_x, 0, keepdims=False)
 
-    def scattered(quarter, q, k, v):
+    def scattered(quarter, far, q, k, v):
+        far = permute(far, BEFORE)
         pieces = exchange(quarter, Y_GROUPS)
         summed, stats = pl.pallas_call(
             own_kernel,
@@ -216,7 +218,7 @@
         pieces, summed, stats = tied(pieces, summed, stats)
         piece = lax.dynamic_index_in_dim(pieces, owner_y, 0, keepdims=False)
         piece = jnp.where(side == owner_z, piece, permute(piece, DIAGONAL))
-        return piece, summed, stats
+        return piece, far, summed, stats
 
     def nothing(function):
         def run(*operands):
@@ -226,29 +228,34 @@
         return run
 
     always = owner[0] >= 0
-    piece, summed, stats = lax.cond(
-        always, scattered, nothing(scattered), quarter, queries, keys, values
-    )
-    column = exchange(copies(piece, NY), Y_GROUPS)
-    far = permute(tied(far, piece)[0], ONWARD)
-    fwd = permute(tied(mid, piece)[0], ONWARD)
-    near = permute(pack(2 - 2 * side)[0], FLIP)
-
-    fan = pl.pallas_call(
-        fan_kernel,
-        grid=(NX,),
-        in_specs=[pl.BlockSpec(column.shape, lambda i: (0, 0, 0, 0))],
-        out_specs=pl.BlockSpec((1,) + column.shape, lambda i: (i, 0, 0, 0, 0)),
-        out_shape=jax.ShapeDtypeStruct((NX,) + column.shape, BF16),
-        cost_estimate=pl.CostEstimate(flops=6 * 10**9, transcendentals=0, bytes_accessed=0),
-        compiler_params=roomy,
-        name="fan_out",
-    )(column)
-
-    def gathered(fan):
-        return exchange(fan, X_GROUPS)
-
-    image = lax.cond(always, gathered, nothing(gathered), fan)
+    piece, far, summed, stats = lax.cond(
+        always, scattered, nothing(scattered), quarter, far, queries, keys, values
+    )
+    far = permute(far, FLIP)
+
+    mid, piece = tied(mid, piece)
+    fwd = permute(mid, ONWARD)
+
+    def gathered(piece):
+        column = exchange(copies(piece, NY), Y_GROUPS)
+        return exchange(copies(column, NX), X_GROUPS)
+
+    image = lax.cond(always, gathered, nothing(gathered), piece)
+
+    def held(stats, arrived):
+        return pl.pallas_call(
+            hold_kernel,
+            in_specs=[pl.BlockSpec(memory_space=pltpu.HBM)] * 2,
+            out_specs=pl.BlockSpec(memory_space=pltpu.HBM),
+            out_shape=state_shape[1],
+            input_output_aliases={0: 0},
+            compiler_params=pltpu.CompilerParams(vmem_limit_bytes=63 * 2**20),
+            cost_estimate=pl.CostEstimate(flops=3 * 10**9, transcendentals=0, bytes_accessed=0),
+            name="hold",
+        )(stats, arrived)
+
+    far, stats = tied(far, held(stats, near))
+    fwd, stats = tied(fwd, held(stats, far))
 
     return pl.pallas_call(
         last_kernel,
@@ -262,7 +269,7 @@
         ),
         out_shape=jax.ShapeDtypeStruct((rows, width), BF16),
         cost_estimate=cost(12, heads),
-        compiler_params=roomy,
+        compiler_params=pltpu.CompilerParams(vmem_limit_bytes=63 * 2**20),
         name="image_and_halo",
     )(sides, mirrored, queries, summed, stats, image, far, mid, fwd, near)
 

time: 137 us -> 125 us (0.912)
  starting transfers between devices: 57.4 us -> 50.4 us
  waiting for transfers between devices: 5.26 us -> 8.97 us
  Pallas kernels: 23.8 us -> 20.7 us
  blocking collectives: 39.2 us -> 37 us
  local copies, waits for them, and re-layouts: 6.73 us -> 4.53 us
    ppermute x6, waiting for transfers between devices: 1.97 us -> 7.09 us  [permute(): return lax.ppermute(value, 'frame', pairs)]
    all_to_all x3 -> x2, starting transfers between devices: 17.9 us -> 13 us  [exchange(): lax.all_to_all(value, 'frame', 0, 0, axis_index_groups=groups, tiled=True)]
    pallas_call x1 -> x2, Pallas kernels: 2.6 us -> 0.01 us  [held(): pl.pallas_call(hold_kernel, in_specs=[pl.BlockSpec(memory_space=pltpu.HBM...]
    all_to_all x1 -> x2, blocking collectives: 39.2 us -> 37 us  [exchange(): lax.all_to_all(value, 'frame', 0, 0, axis_index_groups=groups, tiled=True)]
    ppermute x6, starting transfers between devices: 39.5 us -> 37.5 us  [permute(): return lax.ppermute(value, 'frame', pairs)]
    all_to_all x3 -> x2, waiting for transfers between devices: 3.3 us -> 1.87 us  [exchange(): lax.all_to_all(value, 'frame', 0, 0, axis_index_groups=groups, tiled=True)]
    pallas_call x2 -> x1, Pallas kernels: 2.85 us -> 2.23 us  [pack(): pl.pallas_call(pack_kernel, grid_spec=pltpu.PrefetchScalarGridSpec(num_sc...]
  transfers between devices with their start and end apart: 9 -> 8, of which waited for: 2 -> 3; matrix products, arithmetic and copies ran while one was open for 4% -> 3% of each run, Pallas kernels for 10% -> 8%
where the time goes in v2:
time: 125 us; the launch traced here: 124 us
  starting transfers between devices  50.4 us (40%)
  blocking collectives  37 us (30%)
  Pallas kernels  20.7 us (17%)
  waiting for transfers between devices  8.97 us (7%)
  local copies, waits for them, and re-layouts  4.53 us (4%)
  other arithmetic  1.25 us (1%)
    ppermute x6, starting transfers between devices, permute(): return lax.ppermute(value, 'frame', pairs)  37.5 us
    all_to_all x2, blocking collectives, exchange(): lax.all_to_all(value, 'frame', 0, 0, axis_index_groups=groups, tiled=True)  37 us
    all_to_all x2, starting transfers between devices, exchange(): lax.all_to_all(value, 'frame', 0, 0, axis_index_groups=groups, tiled=True)  13 us
    pallas_call x1, Pallas kernels, per_device(): pl.pallas_call(last_kernel, grid_spec=pltpu.PrefetchScalarGridSpec(num_sc...  10.2 us
    pallas_call x1, Pallas kernels, scattered(): pl.pallas_call(own_kernel, grid=(heads,), in_specs=[smem, every, every, e...  8.3 us
    ppermute x6, waiting for transfers between devices, permute(): return lax.ppermute(value, 'frame', pairs)  7.09 us
    transpose x1, local copies, waits for them, and re-layouts, per_device(): quarters = exchange(jnp.transpose(slot, (1, 2, 0, 3, 4)), X_GROUPS)  2.53 us
  transfers between devices with their start and end apart: 8, of which 3 were waited for; matrix products, arithmetic and copies ran while one was open for 3% of the time, Pallas kernels for 8%

profile of v2, /device:TPU:1, one launch (start us, length us, event | category | flops | bytes accessed | tf_op | source)
XLA Modules:
  0.0 124.4 jit_solution(14146745284553964842)
XLA Ops:
  0.0 2.5 %copy.10 = bf16[4,8,2,16,640]{4,3,1,2,0:T(8,128)(2,1)} copy(bf16[4,8,2,16,640]{4,3,1,0,2:T(8,128)(2,1)} %bitcast.17) | data formatting | bytes 2621440 | tf_op jit(solution)/shard_map/transpose | solution.py:202
  2.5 0.0 copy-start
  2.5 0.0 copy-start.1
  2.5 5.0 %all-to-all-start.3 = ((bf16[4,8,2,16,640]{4,3,1,2,0:T(8,128)(2,1)}), bf16[4,8,2,16,640]{4,3,1,2,0:T(8,128)(2,1)}, u32[]{:S(2)}, u32[]{:S(2)}) async-start(bf16[4,8,2,16,640]{4,3,1,2,0:T(8,128)(2,1)} %copy.10), calls=%async_computation.3 | async-start | bytes 2621440 | tf_op jit(solution)/shard_map/all_to_all | solution.py:37
  7.5 0.7 pad_add_fusion._
  8.2 0.0 copy-done
  8.2 0.0 copy-done.1
  8.2 0.0 copy-start.3
  8.2 0.0 copy-start.2
  8.2 2.2 %pack_tiles.1 = (bf16[2,256,640]{2,1,0:T(8,128)(2,1)}, bf16[2,256,640]{2,1,0:T(8,128)(2,1)}, bf16[2,256,640]{2,1,0:T(8,128)(2,1)}) custom-call(s32[3]{0:T(128)} %pad_add_fusion._, bf16[768,640]{1,0:T(8,128)(2,1)S(1)} %copy-done, bf16[768,640]{1,0:T(8,128)(2,1)S(1)} %copy-done.1, bf16[768,640]{1,0:T(8,128)(2,1)S(1)} %copy-done, ...), custom_call_target="tpu_custom_call" | custom-call | flops 1 | bytes 1 | tf_op jit(solution)/shard_map/pack_tiles/pallas_call | solution.py:173
  10.4 10.9 %collective-permute-start.2 = (bf16[2,256,640]{2,1,0:T(8,128)(2,1)}, bf16[2,256,640]{2,1,0:T(8,128)(2,1)}, u32[]{:S(2)}, u32[]{:S(2)}) collective-permute-start(bf16[2,256,640]{2,1,0:T(8,128)(2,1)} %get-tuple-element.128), channel_id=1, source_target_pairs={{0,8},{8,0},{16,24},{24,16},{32,40},{40,32},{48,56},{56,48},{64,72... | collective-permute-start | bytes 1966088 | tf_op jit(solution)/shard_map/ppermute | solution.py:33
  21.3 1.9 %collective-permute-start.5 = (bf16[2,256,640]{2,1,0:T(8,128)(2,1)}, bf16[2,256,640]{2,1,0:T(8,128)(2,1)}, u32[]{:S(2)}, u32[]{:S(2)}) collective-permute-start(bf16[2,256,640]{2,1,0:T(8,128)(2,1)} %get-tuple-element.133), channel_id=1, source_target_pairs={{0,8},{8,0},{16,24},{24,16},{32,40},{40,32},{48,56},{56,48},{64,72... | collective-permute-start | bytes 1966088 | tf_op jit(solution)/shard_map/ppermute | solution.py:33
  23.9 0.0 copy-done.3
  24.0 0.0 all-to-all-done.3
  24.0 0.0 copy-done.2
  24.0 35.6 %conditional.2 = (bf16[2,16,640]{2,1,0:T(8,128)(2,1)S(1)}, bf16[2,256,640]{2,1,0:T(8,128)(2,1)}, f32[768,640]{1,0:T(8,128)}, f32[768,128]{1,0:T(8,128)}) conditional(s32[]{:T(128)} %convert_element_type.4, () %tuple.37, (pred[]{:T(512)}, s32[]{:T(128)}, s32[]{:T(128)}, pred[]{:T(512)}, s32[]{:T(128)}, ...), branch_computations={%region_0.1_spmd, %region_1.2_spmd} | conditional | flops 20568 | bytes 4629077 | solution.py:231
  24.7 1.7 %dynamic-slice_bitcast_fusion = bf16[8,2,16,640]{3,2,1,0:T(8,128)(2,1)} fusion(s32[]{:T(128)S(6)} %select_n.42, bf16[4,8,2,16,640]{4,3,1,2,0:T(8,128)(2,1)} %get-tuple-element.170), kind=kLoop, calls=%fused_computation | loop fusion | bytes 655364 | tf_op jit(solution)/shard_map/jit(dynamic_index_in_dim)/squeeze | solution.py:203
  26.4 8.0 %all-to-all-start.2 = ((bf16[8,2,16,640]{3,2,1,0:T(8,128)(2,1)}), bf16[8,2,16,640]{3,2,1,0:T(8,128)(2,1)S(1)}, u32[]{:S(2)}, u32[]{:S(2)}) async-start(bf16[8,2,16,640]{3,2,1,0:T(8,128)(2,1)} %dynamic-slice_bitcast_fusion), calls=%async_computation.2 | async-start | bytes 655360 | tf_op jit(solution)/shard_map/cond/branch_1_fun/all_to_all | solution.py:37
  34.4 1.3 %collective-permute-start.1 = (bf16[2,256,640]{2,1,0:T(8,128)(2,1)}, bf16[2,256,640]{2,1,0:T(8,128)(2,1)}, u32[]{:S(2)}, u32[]{:S(2)}) collective-permute-start(bf16[2,256,640]{2,1,0:T(8,128)(2,1)} %get-tuple-element.110), channel_id=1, source_target_pairs={{8,24},{24,40},{40,56},{56,72},{72,88},{88,104},{104,120},{120,136... | collective-permute-start | bytes 1966088 | tf_op jit(solution)/shard_map/cond/branch_1_fun/ppermute | solution.py:33
  35.7 8.3 %own_tiles.1 = (f32[768,640]{1,0:T(8,128)}, f32[768,128]{1,0:T(8,128)}) custom-call(f32[3,5]{1,0:T(4,128)S(1)} %get-tuple-element.102.bias, bf16[768,640]{1,0:T(8,128)(2,1)S(1)} %get-tuple-element.103.q, bf16[768,640]{1,0:T(8,128)(2,1)S(1)} %get-tuple-element.104.k, bf16[768,640]{1,0:T(8,128)(2,1)S(1)} %get-tuple-element.105.v), custom_call_target="tpu_custom_call" | custom-call | flops 45 | bytes 9 | tf_op jit(solution)/shard_map/cond/branch_1_fun/own_tiles/pallas_call | solution.py:208
  44.0 1.9 %all-to-all-done.2 = bf16[8,2,16,640]{3,2,1,0:T(8,128)(2,1)S(1)} async-done(((bf16[8,2,16,640]{3,2,1,0:T(8,128)(2,1)}), bf16[8,2,16,640]{3,2,1,0:T(8,128)(2,1)S(1)}, u32[]{:S(2)}, u32[]{:S(2)}) %all-to-all-start.2) | async-done | bytes 327712 | tf_op jit(solution)/shard_map/cond/branch_1_fun/all_to_all | solution.py:37
  45.8 11.8 %collective-permute-start = (bf16[2,16,640]{2,1,0:T(8,128)(2,1)S(1)}, bf16[2,16,640]{2,1,0:T(8,128)(2,1)S(1)}, u32[]{:S(2)}, u32[]{:S(2)}) collective-permute-start(bf16[2,16,640]{2,1,0:T(8,128)(2,1)S(1)} %dynamic-slice_bitcast_fusion.1), channel_id=1, source_target_pairs={{0,24},{8,112},{16,40},{24,0},{32,56},{40,16},{48,72},{56,32},{64,... | collective-permute-start | bytes 122888 | tf_op jit(solution)/shard_map/cond/branch_1_fun/ppermute | solution.py:33
  57.6 2.0 %collective-permute-done = bf16[2,16,640]{2,1,0:T(8,128)(2,1)S(1)} collective-permute-done((bf16[2,16,640]{2,1,0:T(8,128)(2,1)S(1)}, bf16[2,16,640]{2,1,0:T(8,128)(2,1)S(1)}, u32[]{:S(2)}, u32[]{:S(2)}) %collective-permute-start) | collective-permute-done | bytes 40992 | tf_op jit(solution)/shard_map/cond/branch_1_fun/ppermute | solution.py:33
  59.6 0.0 collective-permute-done.1
  59.6 9.3 %collective-permute-start.4 = (bf16[2,256,640]{2,1,0:T(8,128)(2,1)}, bf16[2,256,640]{2,1,0:T(8,128)(2,1)}, u32[]{:S(2)}, u32[]{:S(2)}) collective-permute-start(bf16[2,256,640]{2,1,0:T(8,128)(2,1)} %get-tuple-element.131), channel_id=1, source_target_pairs={{0,8},{8,0},{16,24},{24,16},{32,40},{40,32},{48,56},{56,48},{64,72... | collective-permute-start | bytes 1966088 | tf_op jit(solution)/shard_map/ppermute | solution.py:33
  68.9 0.1 rev.3
  69.0 0.0 collective-permute-done.2.mid
  69.0 2.3 %collective-permute-start.3 = (bf16[2,256,640]{2,1,0:T(8,128)(2,1)}, bf16[2,256,640]{2,1,0:T(8,128)(2,1)}, u32[]{:S(2)}, u32[]{:S(2)}) collective-permute-start(bf16[2,256,640]{2,1,0:T(8,128)(2,1)} %collective-permute-done.2.mid), channel_id=1, source_target_pairs={{0,16},{16,32},{32,48},{48,64},{64,80},{80,96},{96,112},{112,128},... | collective-permute-start | bytes 1966088 | tf_op jit(solution)/shard_map/ppermute | solution.py:33
  71.3 0.6 broadcast_select_fusion.1.bias
  71.9 37.2 %conditional.3 = (bf16[4,8,2,16,640]{4,3,2,1,0:T(8,128)(2,1)}) conditional(s32[]{:T(128)} %convert_element_type.4, () %tuple.42, bf16[2,16,640]{2,1,0:T(8,128)(2,1)S(1)} %get-tuple-element.137), branch_computations={%region_2.3_spmd, %region_3.4_spmd} | conditional | bytes 5283848 | solution.py:243
  71.9 20.9 %all_to_all.17 = bf16[8,2,16,640]{3,2,1,0:T(8,128)(2,1)S(1)} all-to-all(bf16[8,2,16,640]{3,2,1,0:T(8,128)(2,1)S(1)} %broadcast_in_dim.8), channel_id=1, replica_groups={{0,16,32,48,64,80,96,112},{8,24,40,56,72,88,104,120},{128,144,160,176,1..., dimensions={0} | all-to-all | bytes 655360 | tf_op jit(solution)/shard_map/cond/branch_1_fun/all_to_all | solution.py:37
  92.8 0.1 broadcast_in_dim.9
  92.9 16.2 %all_to_all.18 = bf16[4,8,2,16,640]{4,3,2,1,0:T(8,128)(2,1)} all-to-all(bf16[4,8,2,16,640]{4,3,2,1,0:T(8,128)(2,1)S(1)} %broadcast_in_dim.9), channel_id=1, replica_groups={{0,128,256,384},{8,136,264,392},{16,144,272,400},{24,152,280,408},{32,1..., dimensions={0} | all-to-all | bytes 2621440 | tf_op jit(solution)/shard_map/cond/branch_1_fun/all_to_all | solution.py:37
  109.1 0.0 collective-permute-done.5.arrived.near
  109.1 5.1 %collective-permute-done.4.arrived.far = bf16[2,256,640]{2,1,0:T(8,128)(2,1)} collective-permute-done((bf16[2,256,640]{2,1,0:T(8,128)(2,1)}, bf16[2,256,640]{2,1,0:T(8,128)(2,1)}, u32[]{:S(2)}, u32[]{:S(2)}) %collective-permute-start.4) | collective-permute-done | bytes 655392 | tf_op jit(solution)/shard_map/ppermute | solution.py:33
  114.2 0.0 collective-permute-done.3.fwd
  114.2 10.2 %image_and_halo.1 = bf16[768,640]{1,0:T(8,128)(2,1)} custom-call(s32[1]{0:T(128)} %bitcast.2.side, f32[3,5]{1,0:T(4,128)} %broadcast_select_fusion.1.bias, bf16[768,640]{1,0:T(8,128)(2,1)S(1)} %copy-done.2, f32[768,640]{1,0:T(8,128)} %get-tuple-element.127.summed, f32[768,128]{1,0:T(8,128)} %hold.3.stats, ...), custom_call_target="tpu_custom_call" | custom-call | flops 60 | bytes 12 | tf_op jit(solution)/shard_map/image_and_halo/pallas_call | solution.py:260
  (6 shorter events, 0.0 us)
Async XLA Ops:
  2.5 5.6 %copy-start = (bf16[768,640]{1,0:T(8,128)(2,1)S(1)}, bf16[768,640]{1,0:T(8,128)(2,1)}, u32[]{:S(2)}) copy-start(bf16[768,640]{1,0:T(8,128)(2,1)} %refs_4_.1) | copy-start | bytes 2949124
  2.5 5.6 %copy-start.1 = (bf16[768,640]{1,0:T(8,128)(2,1)S(1)}, bf16[768,640]{1,0:T(8,128)(2,1)}, u32[]{:S(2)}) copy-start(bf16[768,640]{1,0:T(8,128)(2,1)} %refs_5_.1) | copy-start | bytes 2949124
  2.5 21.4 %all-to-all-start.3 = ((bf16[4,8,2,16,640]{4,3,1,2,0:T(8,128)(2,1)}), bf16[4,8,2,16,640]{4,3,1,2,0:T(8,128)(2,1)}, u32[]{:S(2)}, u32[]{:S(2)}) async-start(bf16[4,8,2,16,640]{4,3,1,2,0:T(8,128)(2,1)} %copy.10), calls=%async_computation.3 | async-start | bytes 2621440 | tf_op jit(solution)/shard_map/all_to_all | solution.py:37
  8.2 15.8 %copy-start.3 = (s32[3,5]{1,0:T(4,128)S(1)}, s32[3,5]{1,0:T(4,128)}, u32[]{:S(2)}) copy-start(s32[3,5]{1,0:T(4,128)} %param.15) | copy-start | bytes 184
  8.2 15.8 %copy-start.2 = (bf16[768,640]{1,0:T(8,128)(2,1)S(1)}, bf16[768,640]{1,0:T(8,128)(2,1)}, u32[]{:S(2)}) copy-start(bf16[768,640]{1,0:T(8,128)(2,1)} %q.1) | copy-start | bytes 2949124
  10.4 58.6 %collective-permute-start.2 = (bf16[2,256,640]{2,1,0:T(8,128)(2,1)}, bf16[2,256,640]{2,1,0:T(8,128)(2,1)}, u32[]{:S(2)}, u32[]{:S(2)}) collective-permute-start(bf16[2,256,640]{2,1,0:T(8,128)(2,1)} %get-tuple-element.128), channel_id=1, source_target_pairs={{0,8},{8,0},{16,24},{24,16},{32,40},{40,32},{48,56},{56,48},{64,72... | collective-permute-start | bytes 1966088 | tf_op jit(solution)/shard_map/ppermute | solution.py:33
  21.3 87.7 %collective-permute-start.5 = (bf16[2,256,640]{2,1,0:T(8,128)(2,1)}, bf16[2,256,640]{2,1,0:T(8,128)(2,1)}, u32[]{:S(2)}, u32[]{:S(2)}) collective-permute-start(bf16[2,256,640]{2,1,0:T(8,128)(2,1)} %get-tuple-element.133), channel_id=1, source_target_pairs={{0,8},{8,0},{16,24},{24,16},{32,40},{40,32},{48,56},{56,48},{64,72... | collective-permute-start | bytes 1966088 | tf_op jit(solution)/shard_map/ppermute | solution.py:33
  26.4 19.4 %all-to-all-start.2 = ((bf16[8,2,16,640]{3,2,1,0:T(8,128)(2,1)}), bf16[8,2,16,640]{3,2,1,0:T(8,128)(2,1)S(1)}, u32[]{:S(2)}, u32[]{:S(2)}) async-start(bf16[8,2,16,640]{3,2,1,0:T(8,128)(2,1)} %dynamic-slice_bitcast_fusion), calls=%async_computation.2 | async-start | bytes 655360 | tf_op jit(solution)/shard_map/cond/branch_1_fun/all_to_all | solution.py:37
  34.4 25.2 %collective-permute-start.1 = (bf16[2,256,640]{2,1,0:T(8,128)(2,1)}, bf16[2,256,640]{2,1,0:T(8,128)(2,1)}, u32[]{:S(2)}, u32[]{:S(2)}) collective-permute-start(bf16[2,256,640]{2,1,0:T(8,128)(2,1)} %get-tuple-element.110), channel_id=1, source_target_pairs={{8,24},{24,40},{40,56},{56,72},{72,88},{88,104},{104,120},{120,136... | collective-permute-start | bytes 1966088 | tf_op jit(solution)/shard_map/cond/branch_1_fun/ppermute | solution.py:33
  45.8 13.7 %collective-permute-start = (bf16[2,16,640]{2,1,0:T(8,128)(2,1)S(1)}, bf16[2,16,640]{2,1,0:T(8,128)(2,1)S(1)}, u32[]{:S(2)}, u32[]{:S(2)}) collective-permute-start(bf16[2,16,640]{2,1,0:T(8,128)(2,1)S(1)} %dynamic-slice_bitcast_fusion.1), channel_id=1, source_target_pairs={{0,24},{8,112},{16,40},{24,0},{32,56},{40,16},{48,72},{56,32},{64,... | collective-permute-start | bytes 122888 | tf_op jit(solution)/shard_map/cond/branch_1_fun/ppermute | solution.py:33
  59.6 54.6 %collective-permute-start.4 = (bf16[2,256,640]{2,1,0:T(8,128)(2,1)}, bf16[2,256,640]{2,1,0:T(8,128)(2,1)}, u32[]{:S(2)}, u32[]{:S(2)}) collective-permute-start(bf16[2,256,640]{2,1,0:T(8,128)(2,1)} %get-tuple-element.131), channel_id=1, source_target_pairs={{0,8},{8,0},{16,24},{24,16},{32,40},{40,32},{48,56},{56,48},{64,72... | collective-permute-start | bytes 1966088 | tf_op jit(solution)/shard_map/ppermute | solution.py:33
  69.0 45.2 %collective-permute-start.3 = (bf16[2,256,640]{2,1,0:T(8,128)(2,1)}, bf16[2,256,640]{2,1,0:T(8,128)(2,1)}, u32[]{:S(2)}, u32[]{:S(2)}) collective-permute-start(bf16[2,256,640]{2,1,0:T(8,128)(2,1)} %collective-permute-done.2.mid), channel_id=1, source_target_pairs={{0,16},{16,32},{32,48},{48,64},{64,80},{80,96},{96,112},{112,128},... | collective-permute-start | bytes 1966088 | tf_op jit(solution)/shard_map/ppermute | solution.py:33

commit v3 on v2

--- a/solution.py
+++ b/solution.py
@@ -106,6 +106,16 @@
         refs[2 * count + i][1] = refs[2 * i + 1][...]
 
 
+def fan_kernel(one, out, sems):
+    copies = [
+        pltpu.make_async_copy(one, out.at[i], sems.at[i]) for i in range(out.shape[0])
+    ]
+    for c in copies:
+        c.start()
+    for c in copies:
+        c.wait()
+
+
 def own_kernel(bias, q, k, v, summed_ref, stats_ref):
     h = pl.program_id(0)
     for t in range(3):
@@ -231,16 +241,26 @@
     piece, far, summed, stats = lax.cond(
         always, scattered, nothing(scattered), quarter, far, queries, keys, values
     )
+    column = exchange(copies(piece, NY), Y_GROUPS)
+    column, near = tied(column, near)
+    fwd = permute(tied(mid, piece)[0], ONWARD)
     far = permute(far, FLIP)
 
-    mid, piece = tied(mid, piece)
-    fwd = permute(mid, ONWARD)
-
-    def gathered(piece):
-        column = exchange(copies(piece, NY), Y_GROUPS)
-        return exchange(copies(column, NX), X_GROUPS)
-
-    image = lax.cond(always, gathered, nothing(gathered), piece)
+    fan = pl.pallas_call(
+        fan_kernel,
+        in_specs=[pl.BlockSpec(memory_space=pltpu.VMEM)],
+        out_specs=pl.BlockSpec(memory_space=pltpu.HBM),
+        out_shape=jax.ShapeDtypeStruct((NX,) + column.shape, BF16),
+        scratch_shapes=[pltpu.SemaphoreType.DMA((NX,))],
+        cost_estimate=pl.CostEstimate(flops=6 * 10**9, transcendentals=0, bytes_accessed=0),
+        compiler_params=roomy,
+        name="fan_out",
+    )(column)
+
+    def gathered(fan):
+        return exchange(fan, X_GROUPS)
+
+    image = lax.cond(always, gathered, nothing(gathered), fan)
 
     def held(stats, arrived):
         return pl.pallas_call(
@@ -254,7 +274,6 @@
             name="hold",
         )(stats, arrived)
 
-    far, stats = tied(far, held(stats, near))
     fwd, stats = tied(fwd, held(stats, far))
 
     return pl.pallas_call(

time: 125 us -> 125 us (level)
  blocking collectives: 37 us -> 29.2 us
  starting transfers between devices: 50.4 us -> 57.1 us
  waiting for transfers between devices: 8.97 us -> 7.35 us
  Pallas kernels: 20.7 us -> 22.1 us
  local copies, waits for them, and re-layouts: 4.53 us -> 5.85 us
    all_to_all x2 -> x1, blocking collectives: 37 us -> 29.2 us  [exchange(): lax.all_to_all(value, 'frame', 0, 0, axis_index_groups=groups, tiled=True)]
    all_to_all x2 -> x3, starting transfers between devices: 13 us -> 17.6 us  [exchange(): lax.all_to_all(value, 'frame', 0, 0, axis_index_groups=groups, tiled=True)]
    ppermute x6, starting transfers between devices: 37.5 us -> 39.5 us  [permute(): return lax.ppermute(value, 'frame', pairs)]
    ppermute x6, waiting for transfers between devices: 7.09 us -> 5.48 us  [permute(): return lax.ppermute(value, 'frame', pairs)]
    pallas_call x0 -> x1, Pallas kernels: none -> 1.42 us  [per_device(): pl.pallas_call(fan_kernel, in_specs=[pl.BlockSpec(memory_space=pltpu.VMEM...]
  transfers between devices with their start and end apart: 8 -> 9, of which waited for: 3 -> 3; matrix products, arithmetic and copies ran while one was open for 3% -> 3% of each run, Pallas kernels for 8% -> 10%
where the time goes in v3:
time: 125 us; the launch traced here: 124 us
  starting transfers between devices  57.1 us (46%)
  blocking collectives  29.2 us (23%)
  Pallas kernels  22.1 us (18%)
  waiting for transfers between devices  7.35 us (6%)
  local copies, waits for them, and re-layouts  5.85 us (5%)
    ppermute x6, starting transfers between devices, permute(): return lax.ppermute(value, 'frame', pairs)  39.5 us
    all_to_all x1, blocking collectives, exchange(): lax.all_to_all(value, 'frame', 0, 0, axis_index_groups=groups, tiled=True)  29.2 us
    all_to_all x3, starting transfers between devices, exchange(): lax.all_to_all(value, 'frame', 0, 0, axis_index_groups=groups, tiled=True)  17.6 us
    pallas_call x1, Pallas kernels, per_device(): pl.pallas_call(last_kernel, grid_spec=pltpu.PrefetchScalarGridSpec(num_sc...  10.2 us
    pallas_call x1, Pallas kernels, scattered(): pl.pallas_call(own_kernel, grid=(heads,), in_specs=[smem, every, every, e...  8.31 us
    ppermute x6, waiting for transfers between devices, permute(): return lax.ppermute(value, 'frame', pairs)  5.48 us
    transpose x1, local copies, waits for them, and re-layouts, per_device(): quarters = exchange(jnp.transpose(slot, (1, 2, 0, 3, 4)), X_GROUPS)  2.52 us
  transfers between devices with their start and end apart: 9, of which 3 were waited for; matrix products, arithmetic and copies ran while one was open for 3% of the time, Pallas kernels for 10%

profile of v3, /device:TPU:1, one launch (start us, length us, event | category | flops | bytes accessed | tf_op | source)
XLA Modules:
  0.0 124.4 jit_solution(17593807712154426962)
XLA Ops:
  0.0 2.5 %copy.9 = bf16[4,8,2,16,640]{4,3,1,2,0:T(8,128)(2,1)} copy(bf16[4,8,2,16,640]{4,3,1,0,2:T(8,128)(2,1)} %bitcast.17) | data formatting | bytes 2621440 | tf_op jit(solution)/shard_map/transpose | solution.py:212
  2.5 0.0 copy-start
  2.5 0.0 copy-start.1
  2.5 5.0 %all-to-all-start.2 = ((bf16[4,8,2,16,640]{4,3,1,2,0:T(8,128)(2,1)}), bf16[4,8,2,16,640]{4,3,1,2,0:T(8,128)(2,1)}, u32[]{:S(2)}, u32[]{:S(2)}) async-start(bf16[4,8,2,16,640]{4,3,1,2,0:T(8,128)(2,1)} %copy.9), calls=%async_computation.2 | async-start | bytes 2621440 | tf_op jit(solution)/shard_map/all_to_all | solution.py:37
  7.5 0.6 pad_add_fusion._
  8.1 0.0 copy-done
  8.1 0.0 copy-done.1
  8.1 0.0 copy-start.4
  8.1 0.0 copy-start.2
  8.1 2.2 %pack_tiles.1 = (bf16[2,256,640]{2,1,0:T(8,128)(2,1)}, bf16[2,256,640]{2,1,0:T(8,128)(2,1)}, bf16[2,256,640]{2,1,0:T(8,128)(2,1)}) custom-call(s32[3]{0:T(128)} %pad_add_fusion._, bf16[768,640]{1,0:T(8,128)(2,1)S(1)} %copy-done, bf16[768,640]{1,0:T(8,128)(2,1)S(1)} %copy-done.1, bf16[768,640]{1,0:T(8,128)(2,1)S(1)} %copy-done, ...), custom_call_target="tpu_custom_call" | custom-call | flops 1 | bytes 1 | tf_op jit(solution)/shard_map/pack_tiles/pallas_call | solution.py:183
  10.3 10.9 %collective-permute-start.2 = (bf16[2,256,640]{2,1,0:T(8,128)(2,1)}, bf16[2,256,640]{2,1,0:T(8,128)(2,1)}, u32[]{:S(2)}, u32[]{:S(2)}) collective-permute-start(bf16[2,256,640]{2,1,0:T(8,128)(2,1)} %get-tuple-element.127), channel_id=1, source_target_pairs={{0,8},{8,0},{16,24},{24,16},{32,40},{40,32},{48,56},{56,48},{64,72... | collective-permute-start | bytes 1966088 | tf_op jit(solution)/shard_map/ppermute | solution.py:33
  21.3 1.9 %collective-permute-start.5 = (bf16[2,256,640]{2,1,0:T(8,128)(2,1)}, bf16[2,256,640]{2,1,0:T(8,128)(2,1)}, u32[]{:S(2)}, u32[]{:S(2)}) collective-permute-start(bf16[2,256,640]{2,1,0:T(8,128)(2,1)} %get-tuple-element.133), channel_id=1, source_target_pairs={{0,8},{8,0},{16,24},{24,16},{32,40},{40,32},{48,56},{56,48},{64,72... | collective-permute-start | bytes 1966088 | tf_op jit(solution)/shard_map/ppermute | solution.py:33
  23.2 0.0 copy-done.4
  23.9 0.0 all-to-all-done.2
  23.9 0.0 copy-done.2
  23.9 35.7 %conditional.2 = (bf16[2,16,640]{2,1,0:T(8,128)(2,1)S(1)}, bf16[2,256,640]{2,1,0:T(8,128)(2,1)}, f32[768,640]{1,0:T(8,128)}, f32[768,128]{1,0:T(8,128)}) conditional(s32[]{:T(128)} %convert_element_type.4, () %tuple.37, (pred[]{:T(512)}, s32[]{:T(128)}, s32[]{:T(128)}, pred[]{:T(512)}, s32[]{:T(128)}, ...), branch_computations={%region_0.1_spmd, %region_1.2_spmd} | conditional | flops 20568 | bytes 4629077 | solution.py:241
  24.6 1.7 %dynamic-slice_bitcast_fusion = bf16[8,2,16,640]{3,2,1,0:T(8,128)(2,1)} fusion(s32[]{:T(128)S(6)} %select_n.42, bf16[4,8,2,16,640]{4,3,1,2,0:T(8,128)(2,1)} %get-tuple-element.168), kind=kLoop, calls=%fused_computation | loop fusion | bytes 655364 | tf_op jit(solution)/shard_map/jit(dynamic_index_in_dim)/squeeze | solution.py:213
  26.3 8.0 %all-to-all-start.1 = ((bf16[8,2,16,640]{3,2,1,0:T(8,128)(2,1)}), bf16[8,2,16,640]{3,2,1,0:T(8,128)(2,1)S(1)}, u32[]{:S(2)}, u32[]{:S(2)}) async-start(bf16[8,2,16,640]{3,2,1,0:T(8,128)(2,1)} %dynamic-slice_bitcast_fusion), calls=%async_computation.1 | async-start | bytes 655360 | tf_op jit(solution)/shard_map/cond/branch_1_fun/all_to_all | solution.py:37
  34.4 1.3 %collective-permute-start.1 = (bf16[2,256,640]{2,1,0:T(8,128)(2,1)}, bf16[2,256,640]{2,1,0:T(8,128)(2,1)}, u32[]{:S(2)}, u32[]{:S(2)}) collective-permute-start(bf16[2,256,640]{2,1,0:T(8,128)(2,1)} %get-tuple-element.110), channel_id=1, source_target_pairs={{8,24},{24,40},{40,56},{56,72},{72,88},{88,104},{104,120},{120,136... | collective-permute-start | bytes 1966088 | tf_op jit(solution)/shard_map/cond/branch_1_fun/ppermute | solution.py:33
  35.7 8.3 %own_tiles.1 = (f32[768,640]{1,0:T(8,128)}, f32[768,128]{1,0:T(8,128)}) custom-call(f32[3,5]{1,0:T(4,128)S(1)} %get-tuple-element.102.bias, bf16[768,640]{1,0:T(8,128)(2,1)S(1)} %get-tuple-element.103.q, bf16[768,640]{1,0:T(8,128)(2,1)S(1)} %get-tuple-element.104.k, bf16[768,640]{1,0:T(8,128)(2,1)S(1)} %get-tuple-element.105.v), custom_call_target="tpu_custom_call" | custom-call | flops 45 | bytes 9 | tf_op jit(solution)/shard_map/cond/branch_1_fun/own_tiles/pallas_call | solution.py:218
  44.0 1.9 %all-to-all-done.1 = bf16[8,2,16,640]{3,2,1,0:T(8,128)(2,1)S(1)} async-done(((bf16[8,2,16,640]{3,2,1,0:T(8,128)(2,1)}), bf16[8,2,16,640]{3,2,1,0:T(8,128)(2,1)S(1)}, u32[]{:S(2)}, u32[]{:S(2)}) %all-to-all-start.1) | async-done | bytes 327712 | tf_op jit(solution)/shard_map/cond/branch_1_fun/all_to_all | solution.py:37
  45.8 11.8 %collective-permute-start = (bf16[2,16,640]{2,1,0:T(8,128)(2,1)S(1)}, bf16[2,16,640]{2,1,0:T(8,128)(2,1)S(1)}, u32[]{:S(2)}, u32[]{:S(2)}) collective-permute-start(bf16[2,16,640]{2,1,0:T(8,128)(2,1)S(1)} %dynamic-slice_bitcast_fusion.1), channel_id=1, source_target_pairs={{0,24},{8,112},{16,40},{24,0},{32,56},{40,16},{48,72},{56,32},{64,... | collective-permute-start | bytes 122888 | tf_op jit(solution)/shard_map/cond/branch_1_fun/ppermute | solution.py:33
  57.6 2.0 %collective-permute-done = bf16[2,16,640]{2,1,0:T(8,128)(2,1)S(1)} collective-permute-done((bf16[2,16,640]{2,1,0:T(8,128)(2,1)S(1)}, bf16[2,16,640]{2,1,0:T(8,128)(2,1)S(1)}, u32[]{:S(2)}, u32[]{:S(2)}) %collective-permute-start) | collective-permute-done | bytes 40992 | tf_op jit(solution)/shard_map/cond/branch_1_fun/ppermute | solution.py:33
  59.6 0.0 collective-permute-done.1
  59.6 0.8 broadcast_in_dim.16
  60.3 4.6 %all-to-all-start.3 = ((bf16[8,2,16,640]{3,2,1,0:T(8,128)(2,1)}), bf16[8,2,16,640]{3,2,1,0:T(8,128)(2,1)S(1)}, u32[]{:S(2)}, u32[]{:S(2)}) async-start(bf16[8,2,16,640]{3,2,1,0:T(8,128)(2,1)} %broadcast_in_dim.16), calls=%async_computation.3 | async-start | bytes 655360 | tf_op jit(solution)/shard_map/all_to_all | solution.py:37
  64.9 0.1 rev.3
  65.0 9.4 %collective-permute-start.4 = (bf16[2,256,640]{2,1,0:T(8,128)(2,1)}, bf16[2,256,640]{2,1,0:T(8,128)(2,1)}, u32[]{:S(2)}, u32[]{:S(2)}) collective-permute-start(bf16[2,256,640]{2,1,0:T(8,128)(2,1)} %get-tuple-element.131), channel_id=1, source_target_pairs={{0,8},{8,0},{16,24},{24,16},{32,40},{40,32},{48,56},{56,48},{64,72... | collective-permute-start | bytes 1966088 | tf_op jit(solution)/shard_map/ppermute | solution.py:33
  74.4 0.6 broadcast_select_fusion.1.bias
  75.0 0.0 collective-permute-done.2.mid
  75.0 4.2 %collective-permute-start.3 = (bf16[2,256,640]{2,1,0:T(8,128)(2,1)}, bf16[2,256,640]{2,1,0:T(8,128)(2,1)}, u32[]{:S(2)}, u32[]{:S(2)}) collective-permute-start(bf16[2,256,640]{2,1,0:T(8,128)(2,1)} %collective-permute-done.2.mid), channel_id=1, source_target_pairs={{0,16},{16,32},{32,48},{48,64},{64,80},{80,96},{96,112},{112,128},... | collective-permute-start | bytes 1966088 | tf_op jit(solution)/shard_map/ppermute | solution.py:33
  79.3 0.0 collective-permute-done.5.near
  79.3 0.0 all-to-all-done.3.one
  79.3 0.0 copy-start.3
  79.3 0.7 copy-done.3
  80.0 1.4 %fan_out.1 = bf16[4,8,2,16,640]{4,3,2,1,0:T(8,128)(2,1)S(1)} custom-call(bf16[8,2,16,640]{3,2,1,0:T(8,128)(2,1)} %copy-done.3), custom_call_target="tpu_custom_call" | custom-call | flops 6000000000 | tf_op jit(solution)/shard_map/fan_out/pallas_call | solution.py:249
  81.4 29.2 %conditional.3 = (bf16[4,8,2,16,640]{4,3,2,1,0:T(8,128)(2,1)}) conditional(s32[]{:T(128)} %convert_element_type.4, () %tuple.41, bf16[4,8,2,16,640]{4,3,2,1,0:T(8,128)(2,1)S(1)} %fan_out.1), branch_computations={%region_2.3_spmd, %region_3.4_spmd} | conditional | bytes 2621448 | solution.py:263
  81.4 29.2 %all_to_all.18 = bf16[4,8,2,16,640]{4,3,2,1,0:T(8,128)(2,1)} all-to-all(bf16[4,8,2,16,640]{4,3,2,1,0:T(8,128)(2,1)S(1)} %param.3), channel_id=1, replica_groups={{0,128,256,384},{8,136,264,392},{16,144,272,400},{24,152,280,408},{32,1..., dimensions={0} | all-to-all | bytes 2621440 | tf_op jit(solution)/shard_map/cond/branch_1_fun/all_to_all | solution.py:37
  110.6 3.5 %collective-permute-done.4.arrived.far = bf16[2,256,640]{2,1,0:T(8,128)(2,1)} collective-permute-done((bf16[2,256,640]{2,1,0:T(8,128)(2,1)}, bf16[2,256,640]{2,1,0:T(8,128)(2,1)}, u32[]{:S(2)}, u32[]{:S(2)}) %collective-permute-start.4) | collective-permute-done | bytes 655392 | tf_op jit(solution)/shard_map/ppermute | solution.py:33
  114.2 0.0 collective-permute-done.3.fwd
  114.2 10.2 %image_and_halo.1 = bf16[768,640]{1,0:T(8,128)(2,1)} custom-call(s32[1]{0:T(128)} %bitcast.2.side, f32[3,5]{1,0:T(4,128)} %broadcast_select_fusion.1.bias, bf16[768,640]{1,0:T(8,128)(2,1)S(1)} %copy-done.2, f32[768,640]{1,0:T(8,128)} %get-tuple-element.126.summed, f32[768,128]{1,0:T(8,128)} %hold.1.stats, ...), custom_call_target="tpu_custom_call" | custom-call | flops 60 | bytes 12 | tf_op jit(solution)/shard_map/image_and_halo/pallas_call | solution.py:279
  (4 shorter events, 0.0 us)
Async XLA Ops:
  2.5 5.6 %copy-start = (bf16[768,640]{1,0:T(8,128)(2,1)S(1)}, bf16[768,640]{1,0:T(8,128)(2,1)}, u32[]{:S(2)}) copy-start(bf16[768,640]{1,0:T(8,128)(2,1)} %refs_4_.1) | copy-start | bytes 2949124
  2.5 5.6 %copy-start.1 = (bf16[768,640]{1,0:T(8,128)(2,1)S(1)}, bf16[768,640]{1,0:T(8,128)(2,1)}, u32[]{:S(2)}) copy-start(bf16[768,640]{1,0:T(8,128)(2,1)} %refs_5_.1) | copy-start | bytes 2949124
  2.5 21.4 %all-to-all-start.2 = ((bf16[4,8,2,16,640]{4,3,1,2,0:T(8,128)(2,1)}), bf16[4,8,2,16,640]{4,3,1,2,0:T(8,128)(2,1)}, u32[]{:S(2)}, u32[]{:S(2)}) async-start(bf16[4,8,2,16,640]{4,3,1,2,0:T(8,128)(2,1)} %copy.9), calls=%async_computation.2 | async-start | bytes 2621440 | tf_op jit(solution)/shard_map/all_to_all | solution.py:37
  8.1 15.1 %copy-start.4 = (s32[3,5]{1,0:T(4,128)S(1)}, s32[3,5]{1,0:T(4,128)}, u32[]{:S(2)}) copy-start(s32[3,5]{1,0:T(4,128)} %param.15) | copy-start | bytes 184
  8.1 15.8 %copy-start.2 = (bf16[768,640]{1,0:T(8,128)(2,1)S(1)}, bf16[768,640]{1,0:T(8,128)(2,1)}, u32[]{:S(2)}) copy-start(bf16[768,640]{1,0:T(8,128)(2,1)} %q.1) | copy-start | bytes 2949124
  10.3 64.7 %collective-permute-start.2 = (bf16[2,256,640]{2,1,0:T(8,128)(2,1)}, bf16[2,256,640]{2,1,0:T(8,128)(2,1)}, u32[]{:S(2)}, u32[]{:S(2)}) collective-permute-start(bf16[2,256,640]{2,1,0:T(8,128)(2,1)} %get-tuple-element.127), channel_id=1, source_target_pairs={{0,8},{8,0},{16,24},{24,16},{32,40},{40,32},{48,56},{56,48},{64,72... | collective-permute-start | bytes 1966088 | tf_op jit(solution)/shard_map/ppermute | solution.py:33
  21.3 58.0 %collective-permute-start.5 = (bf16[2,256,640]{2,1,0:T(8,128)(2,1)}, bf16[2,256,640]{2,1,0:T(8,128)(2,1)}, u32[]{:S(2)}, u32[]{:S(2)}) collective-permute-start(bf16[2,256,640]{2,1,0:T(8,128)(2,1)} %get-tuple-element.133), channel_id=1, source_target_pairs={{0,8},{8,0},{16,24},{24,16},{32,40},{40,32},{48,56},{56,48},{64,72... | collective-permute-start | bytes 1966088 | tf_op jit(solution)/shard_map/ppermute | solution.py:33
  26.3 19.5 %all-to-all-start.1 = ((bf16[8,2,16,640]{3,2,1,0:T(8,128)(2,1)}), bf16[8,2,16,640]{3,2,1,0:T(8,128)(2,1)S(1)}, u32[]{:S(2)}, u32[]{:S(2)}) async-start(bf16[8,2,16,640]{3,2,1,0:T(8,128)(2,1)} %dynamic-slice_bitcast_fusion), calls=%async_computation.1 | async-start | bytes 655360 | tf_op jit(solution)/shard_map/cond/branch_1_fun/all_to_all | solution.py:37
  34.4 25.2 %collective-permute-start.1 = (bf16[2,256,640]{2,1,0:T(8,128)(2,1)}, bf16[2,256,640]{2,1,0:T(8,128)(2,1)}, u32[]{:S(2)}, u32[]{:S(2)}) collective-permute-start(bf16[2,256,640]{2,1,0:T(8,128)(2,1)} %get-tuple-element.110), channel_id=1, source_target_pairs={{8,24},{24,40},{40,56},{56,72},{72,88},{88,104},{104,120},{120,136... | collective-permute-start | bytes 1966088 | tf_op jit(solution)/shard_map/cond/branch_1_fun/ppermute | solution.py:33
  45.8 13.7 %collective-permute-start = (bf16[2,16,640]{2,1,0:T(8,128)(2,1)S(1)}, bf16[2,16,640]{2,1,0:T(8,128)(2,1)S(1)}, u32[]{:S(2)}, u32[]{:S(2)}) collective-permute-start(bf16[2,16,640]{2,1,0:T(8,128)(2,1)S(1)} %dynamic-slice_bitcast_fusion.1), channel_id=1, source_target_pairs={{0,24},{8,112},{16,40},{24,0},{32,56},{40,16},{48,72},{56,32},{64,... | collective-permute-start | bytes 122888 | tf_op jit(solution)/shard_map/cond/branch_1_fun/ppermute | solution.py:33
  60.3 18.9 %all-to-all-start.3 = ((bf16[8,2,16,640]{3,2,1,0:T(8,128)(2,1)}), bf16[8,2,16,640]{3,2,1,0:T(8,128)(2,1)S(1)}, u32[]{:S(2)}, u32[]{:S(2)}) async-start(bf16[8,2,16,640]{3,2,1,0:T(8,128)(2,1)} %broadcast_in_dim.16), calls=%async_computation.3 | async-start | bytes 655360 | tf_op jit(solution)/shard_map/all_to_all | solution.py:37
  65.0 49.1 %collective-permute-start.4 = (bf16[2,256,640]{2,1,0:T(8,128)(2,1)}, bf16[2,256,640]{2,1,0:T(8,128)(2,1)}, u32[]{:S(2)}, u32[]{:S(2)}) collective-permute-start(bf16[2,256,640]{2,1,0:T(8,128)(2,1)} %get-tuple-element.131), channel_id=1, source_target_pairs={{0,8},{8,0},{16,24},{24,16},{32,40},{40,32},{48,56},{56,48},{64,72... | collective-permute-start | bytes 1966088 | tf_op jit(solution)/shard_map/ppermute | solution.py:33
  75.0 39.1 %collective-permute-start.3 = (bf16[2,256,640]{2,1,0:T(8,128)(2,1)}, bf16[2,256,640]{2,1,0:T(8,128)(2,1)}, u32[]{:S(2)}, u32[]{:S(2)}) collective-permute-start(bf16[2,256,640]{2,1,0:T(8,128)(2,1)} %collective-permute-done.2.mid), channel_id=1, source_target_pairs={{0,16},{16,32},{32,48},{48,64},{64,80},{80,96},{96,112},{112,128},... | collective-permute-start | bytes 1966088 | tf_op jit(solution)/shard_map/ppermute | solution.py:33
  79.3 0.7 copy-start.3
